TPU v7x, 128 devices: a whole 4x4x4 slice. The times are simulated.
128 devices in a mesh: fibre: 4 (over x), tm: 4 (over z_hi, core), rep: 8 (over z_lo, y).
Axes of the slice: x: 4, y: 4, z: 4 (z_hi: 2, z_lo: 2; z = z_hi * 2 + z_lo), core: 2. Of those that a mesh axis runs over, the one named last changes fastest.
Arguments:
- records: bfloat16 [8, 64, 2048, 128], P('rep', 'fibre', 'tm'), may hold values from -6 to 6
- time_weight: bfloat16 [9, 128, 128], replicated, may hold values from -0.1875 to 0.1875
- fibre_weight: bfloat16 [9, 128, 128], replicated, may hold values from -0.1875 to 0.1875
- cotangent: bfloat16 [8, 64, 2048, 128], P('rep', 'fibre', 'tm'), may hold values from -6 to 6
Outputs:
- mixed: bfloat16 [8, 64, 2048, 128], P('rep', 'fibre', 'tm')
- d_records: bfloat16 [8, 64, 2048, 128], P('rep', 'fibre', 'tm')
- grad_time: float32 [9, 128, 128], replicated
- grad_fibre: float32 [9, 128, 128], replicated
All inputs are finite; a program needn't handle non-finite values.
Results may differ from a plain program's by a relative error of at most 0.0032.
Values may be sent and summed in bfloat16 or wider, within the bound.
A program may use at most 256 MiB of HBM per device.

v0:
```python
import functools

import jax
import jax.numpy as jnp
from jax import lax
from jax.experimental import pallas as pl
from jax.experimental.pallas import tpu as pltpu
from jax.sharding import PartitionSpec as P

MESH = pl.DeviceIdType.MESH
BF, F32 = jnp.bfloat16, jnp.float32
TILE = 4
UNROLL = 2
CHUNKS = 4


def dot(a, b):
    return jnp.dot(a, b, preferred_element_type=F32)


def loop(low, high, body):
    lax.fori_loop(low, high, lambda i, c: (body(i), c)[1], 0, unroll=min(UNROLL, high - low))


def aligned(index, size):
    return pl.ds(pl.multiple_of(index * size, size), size)


def pair_weights(dst, block):
    zero = jnp.zeros((128, 128), BF)
    for b in range(5):
        top, low = slice(256 * b, 256 * b + 128), slice(256 * b + 128, 256 * b + 256)
        dst[top, 0:128] = block(2 * b)
        dst[top, 128:256] = block(2 * b - 1) if b > 0 else zero
        dst[low, 0:128] = block(2 * b + 1) if b < 4 else zero
        dst[low, 128:256] = block(2 * b)


def to_time_pairs(src, q):
    v = src[:, aligned(q, 16), :].astype(F32)
    lo, hi = v[:, 0:8].reshape(128, 128), v[:, 8:16].reshape(128, 128)
    return jnp.concatenate([lo, hi], axis=1).astype(BF)


def natural(y):
    y = y.reshape(16, 8, 256)
    return jnp.concatenate([y[:, :, :128], y[:, :, 128:]], axis=1)


def time_conv(src, w, q0):
    lhs = [src[pl.ds(q0 + b, TILE)].reshape(TILE * 128, 256) for b in range(5)]
    return dot(jnp.concatenate(lhs, axis=1), w[...])


def fibre_conv(src, w, pair, at):
    v = src[pl.ds(2 * pair, 10), at, :]
    return dot(jnp.concatenate([v[i] for i in range(10)], axis=1), w[...])


def do_hidden(xt, w, h, slope, q0):
    y = time_conv(xt, w, q0)
    s = 0.5 * jnp.tanh(0.5 * y) + 0.5
    hid = y * s
    slope[pl.ds(q0, TILE)] = (s + hid * (1.0 - s)).reshape(TILE, 128, 256)
    for j in range(TILE):
        h[4:20, aligned(q0 + j, 16), :] = natural(hid[128 * j : 128 * j + 128]).astype(BF)


def do_d_pre(g, w, slope, dp, pair, chunk, span):
    y = fibre_conv(g, w, pair, aligned(chunk, span)).reshape(span // 8, 8, 256)
    z = jnp.concatenate([y[:, :, :128], y[:, :, 128:]], axis=1).reshape(span // 16, 2, 16, 128)
    z = jnp.concatenate([z[:, 0], z[:, 1]], axis=2)
    rows, q0 = aligned(pair, 16), chunk * (span // 16)
    dp[pl.ds(2 + q0, span // 16), rows, :] = (z * slope[pl.ds(q0, span // 16), rows, :]).astype(BF)


def do_grad_time(xtt, dp, acc, q0, count):
    lhs = [jnp.concatenate([xtt[q0 + b + j] for j in range(count)], axis=1) for b in range(5)]
    acc[...] += dot(jnp.concatenate(lhs, axis=0), dp[pl.ds(2 + q0, count)].reshape(count * 128, 256))


def do_grad_fibre(gt, h, acc, pair):
    lhs = gt[pl.ds(pair, 5)].reshape(1280, gt.shape[2])
    acc[...] += dot(lhs, jnp.concatenate([h[4 + 2 * pair], h[5 + 2 * pair]], axis=1))


def do_d_records(dp, w, g, out, q0):
    y = time_conv(dp, w, q0)
    for j in range(TILE):
        at = aligned(q0 + j, 16)
        out[:, at, :] = (g[4:20, at, :].astype(F32) + natural(y[128 * j : 128 * j + 128])).astype(BF)


def do_mixed(h, w, x, out, pair, at):
    y = fibre_conv(h, w, pair, at)
    out[2 * pair, at] = (x[2 * pair, at].astype(F32) + y[:, :128]).astype(BF)
    out[2 * pair + 1, at] = (x[2 * pair + 1, at].astype(F32) + y[:, 128:]).astype(BF)


def fold(acc, grads):
    def part(i, b, e, d):
        return acc[i, 256 * b + 128 * e : 256 * b + 128 * e + 128, 128 * d : 128 * d + 128]

    for k in range(9):
        if k % 2 == 0:
            low, high = k // 2, (8 - k) // 2
            grads[0, k] = part(0, low, 0, 0) + part(0, low, 1, 1)
            grads[1, k] = (part(1, high, 0, 0) + part(1, high, 1, 1)).T
        else:
            grads[0, k] = part(0, (k - 1) // 2, 1, 0) + part(0, (k + 1) // 2, 0, 1)
            grads[1, k] = (part(1, (9 - k) // 2, 0, 1) + part(1, (7 - k) // 2, 1, 0)).T


def kernel(factor, x_hbm, tw_hbm, fw_hbm, g_hbm, mixed, d_rec, gt_out, gf_out,
           x, g, h, xt, xtt, gt, dp, slope, mix, drec, wraw, big, acc, grads, other, parts, inbox, planes, gathered,
           lsem, gsend, grecv, hsend, hrecv, xsend, xrecv, dsend, drecv, asem, bsend, brecv, csend, crecv, esend, erecv,
           fsem):
    fi, ti, ri = lax.axis_index("fibre"), lax.axis_index("tm"), lax.axis_index("rep")
    nf, nt, nr = lax.axis_size("fibre"), lax.axis_size("tm"), lax.axis_size("rep")
    core = lax.rem(ti, 2)
    members = (nt // 2) * nr
    me = lax.div(ti, 2) * nr + ri
    rows = 128 // members
    used = 9 * rows

    def member(index):
        return {"tm": 2 * lax.div(index, nr) + core, "rep": lax.rem(index, nr)}

    def shifted(axis, index, count, step):
        return {axis: lax.rem(index + step + count, count)}

    partner = {"tm": ti + 1 - 2 * core}

    x_edges = [pltpu.make_async_copy(x_hbm.at[:, at, :], x.at[:, at, :], lsem.at[i])
               for i, at in enumerate((slice(0, 32), slice(480, 512)))]
    x_rest = pltpu.make_async_copy(x_hbm.at[:, 32:480, :], x.at[:, 32:480, :], lsem.at[2])
    w_time = pltpu.make_async_copy(tw_hbm, wraw.at[0], lsem.at[3])
    w_fibre = pltpu.make_async_copy(fw_hbm, wraw.at[1], lsem.at[4])
    g_load = pltpu.make_async_copy(g_hbm, g.at[4:20], lsem.at[5])
    for c in (*x_edges, w_time, x_rest, w_fibre, g_load):
        c.start()

    barrier = pltpu.get_barrier_semaphore()
    others = [shifted("fibre", fi, nf, d) for d in range(1, nf)]
    others += [shifted("tm", ti, nt, d) for d in (1, -1)]
    others += [member(lax.rem(me + d, members)) for d in range(1, members)]
    for d in others:
        pl.semaphore_signal(barrier, inc=1, device_id=d, device_id_type=MESH)
    pl.semaphore_wait(barrier, len(others))

    class Halo:
        def __init__(self, axis, index, count, pieces, send, recv):
            self.has = (index < count - 1, index > 0)
            self.copies = [
                [pltpu.make_async_remote_copy(
                    src_ref=src, dst_ref=dst, send_sem=send.at[side, i], recv_sem=recv.at[side, i],
                    device_id=shifted(axis, index, count, 1 - 2 * side), device_id_type=MESH)
                 for side, (src, dst) in enumerate(piece)]
                for i, piece in enumerate(pieces)]

        def start(self, i):
            for side in range(2):
                pl.when(self.has[side])(self.copies[i][side].start)

        def wait_recv(self, i):
            for side in range(2):
                pl.when(self.has[1 - side])(self.copies[i][side].wait_recv)

        def wait_send(self, i):
            for side in range(2):
                pl.when(self.has[side])(self.copies[i][side].wait_send)

    span = 512 // CHUNKS
    times = [slice(span * i, span * i + span) for i in range(CHUNKS)]
    g_halo = Halo("fibre", fi, nf, [
        ((g_hbm.at[12:16, at, :], g.at[0:4, at, :]), (g_hbm.at[0:4, at, :], g.at[20:24, at, :])) for at in times
    ], gsend, grecv)
    h_halo = Halo("fibre", fi, nf, [
        ((h.at[16:20, at, :], h.at[0:4, at, :]), (h.at[4:8, at, :], h.at[20:24, at, :])) for at in times
    ], hsend, hrecv)
    x_halo = Halo("tm", ti, nt, [((xt.at[32:34], xt.at[0:2]), (xt.at[2:4], xt.at[34:36]))], xsend, xrecv)
    d_halo = Halo("tm", ti, nt, [((dp.at[32:34], dp.at[0:2]), (dp.at[2:4], dp.at[34:36]))], dsend, drecv)
    for i in range(CHUNKS):
        g_halo.start(i)

    def build(q):
        v = to_time_pairs(x, q)
        xt[q + 2] = v
        xtt[q + 2] = v.T

    for c in x_edges:
        c.wait()
    for q in (0, 1, 30, 31):
        build(q)
    x_halo.start(0)

    for edge, at, time_at in ((0, slice(0, 4), slice(0, 2)), (1, slice(20, 24), slice(34, 36))):
        @pl.when((fi == 0) if edge == 0 else (fi == nf - 1))
        def _(at=at):
            g[at] = jnp.zeros((4, 512, 128), BF)
            h[at] = jnp.zeros((4, 512, 128), BF)

        @pl.when((ti == 0) if edge == 0 else (ti == nt - 1))
        def _(at=time_at):
            xt[at] = jnp.zeros((2, 128, 256), BF)
            dp[at] = jnp.zeros((2, 128, 256), BF)

    w_time.wait()
    pair_weights(big.at[0], lambda k: wraw[0, k])
    x_rest.wait()
    loop(2, 30, build)
    last = 32 // TILE - 1
    loop(1, last, lambda i: do_hidden(xt, big.at[0], h, slope, i * TILE))

    w_fibre.wait()
    pair_weights(big.at[1], lambda k: wraw[1, 8 - k].T)
    pair_weights(big.at[2], lambda k: wraw[1, k])
    pair_weights(big.at[3], lambda k: wraw[0, 8 - k].T)

    x_halo.wait_recv(0)
    for q in (0, 1, 34, 35):
        xtt[q] = xt[q].T
    do_hidden(xt, big.at[0], h, slope, last * TILE)
    do_hidden(xt, big.at[0], h, slope, 0)

    g_load.wait()

    def turn(p):
        for at in (slice(0, 128), slice(128, 256), slice(256, 384), slice(384, 512)):
            gt[p, :, at] = jnp.concatenate([g[2 * p, at], g[2 * p + 1, at]], axis=1).T

    acc[...] = jnp.zeros(acc.shape, F32)
    loop(2, 10, turn)
    loop(2, 6, lambda p: do_d_pre(g, big.at[1], slope, dp, p, 0, 512))
    loop(2, 6, lambda p: do_grad_fibre(gt, h, acc.at[1], p))
    loop(2, 6, lambda p: do_mixed(h, big.at[2], x, mix, p, slice(0, 512)))

    for i in range(CHUNKS):
        g_halo.wait_recv(i)
    for i in range(CHUNKS):
        h_halo.start(i)
    for p in (0, 1, 6, 7):
        do_d_pre(g, big.at[1], slope, dp, p, 0, 512)
    d_halo.start(0)
    loop(0, 8, lambda i: do_grad_time(xtt, dp, acc.at[0], 4 * i, 4))
    for p in (0, 1, 10, 11):
        turn(p)
    for p in (0, 1, 6, 7):
        do_grad_fibre(gt, h, acc.at[1], p)
    fold(acc, grads)

    swap = pltpu.make_async_remote_copy(
        src_ref=grads.at[1 - core], dst_ref=other, send_sem=asem.at[0], recv_sem=asem.at[1],
        device_id=partner, device_id_type=MESH)
    swap.start()
    loop(1, last, lambda i: do_d_records(dp, big.at[3], g, drec, i * TILE))
    swap.wait_recv()

    pad = jnp.zeros((parts.shape[1] - used, 128), F32) if parts.shape[1] > used else None

    def padded(v):
        return v if pad is None else jnp.concatenate([v, pad], axis=0)

    for s in range(members):
        at = slice(rows * s, rows * s + rows)
        parts[s] = padded((grads[core, :, at] + other[:, at]).reshape(used, 128)).astype(BF)
    mine = aligned(me, rows)
    own = (grads[core, :, mine] + other[:, mine]).reshape(used, 128)
    scatter = []
    for d in range(1, members):
        to = lax.rem(me + d, members)
        scatter.append(pltpu.make_async_remote_copy(
            src_ref=parts.at[to], dst_ref=inbox.at[d], send_sem=bsend.at[d], recv_sem=brecv.at[d],
            device_id=member(to), device_id_type=MESH))
    for c in scatter:
        c.start()

    d_halo.wait_recv(0)
    do_d_records(dp, big.at[3], g, drec, last * TILE)
    do_d_records(dp, big.at[3], g, drec, 0)
    out_d = pltpu.make_async_copy(drec, d_rec, lsem.at[6])
    out_d.start()

    for d, c in enumerate(scatter, 1):
        c.wait_recv()
        own = own + inbox[d].astype(F32)[:used]
    planes[fi] = own
    spread = []
    for d in range(1, nf):
        to = lax.rem(fi + d, nf)
        spread.append(pltpu.make_async_remote_copy(
            src_ref=planes.at[fi], dst_ref=planes.at[fi], send_sem=csend.at[d], recv_sem=crecv.at[d],
            device_id={"fibre": to}, device_id_type=MESH))
    for c in spread:
        c.start()

    for p in (0, 1, 6, 7):
        pass
    for d in range(1, nf):
        source = lax.rem(fi - d + nf, nf)
        pltpu.make_async_remote_copy(
            src_ref=planes.at[source], dst_ref=planes.at[source], send_sem=csend.at[d], recv_sem=crecv.at[d],
            device_id={"fibre": source}, device_id_type=MESH).wait_recv()
    total = planes[0]
    for i in range(1, nf):
        total = total + planes[i]
    gathered[core, me] = padded(total * factor).astype(BF)
    gather = []
    for d in range(1, members):
        gather.append(pltpu.make_async_remote_copy(
            src_ref=gathered.at[core, me], dst_ref=gathered.at[core, me], send_sem=esend.at[d], recv_sem=erecv.at[d],
            device_id=member(lax.rem(me + d, members)), device_id_type=MESH))
    for c in gather:
        c.start()

    for i in range(CHUNKS):
        h_halo.wait_recv(i)
        for p in (0, 1, 6, 7):
            do_mixed(h, big.at[2], x, mix, p, times[i])
    out_m = pltpu.make_async_copy(mix, mixed, lsem.at[7])
    out_m.start()

    for d in range(1, members):
        source = lax.rem(me - d + members, members)
        pltpu.make_async_remote_copy(
            src_ref=gathered.at[core, source], dst_ref=gathered.at[core, source], send_sem=esend.at[d],
            recv_sem=erecv.at[d], device_id=member(source), device_id_type=MESH).wait_recv()
    final = pltpu.make_async_remote_copy(
        src_ref=gathered.at[core], dst_ref=gathered.at[core], send_sem=fsem.at[0], recv_sem=fsem.at[1],
        device_id=partner, device_id_type=MESH)
    final.start()
    final.wait_send()
    pltpu.make_async_remote_copy(
        src_ref=gathered.at[1 - core], dst_ref=gathered.at[1 - core], send_sem=fsem.at[0], recv_sem=fsem.at[1],
        device_id=partner, device_id_type=MESH).wait_recv()
    for i, out in enumerate((gt_out, gf_out)):
        for s in range(members):
            out[:, rows * s : rows * s + rows] = gathered[i, s].astype(F32)[:used].reshape(9, rows, 128)

    swap.wait_send()
    for c in (*scatter, *spread, *gather):
        c.wait_send()
    for halo, count in ((g_halo, CHUNKS), (h_halo, CHUNKS), (x_halo, 1), (d_halo, 1)):
        for i in range(count):
            halo.wait_send(i)
    out_d.wait()
    out_m.wait()


def shards(factor, records, time_weight, fibre_weight, cotangent):
    nf, nt, nr = lax.axis_size("fibre"), lax.axis_size("tm"), lax.axis_size("rep")
    members = (nt // 2) * nr
    used = 9 * (128 // members)
    height = -(-used // 16) * 16
    dma = pltpu.SemaphoreType.DMA
    any_space, vmem = pl.BlockSpec(memory_space=pl.ANY), pl.BlockSpec(memory_space=pltpu.VMEM)
    field = jax.ShapeDtypeStruct((16, 512, 128), BF)
    grad = jax.ShapeDtypeStruct((9, 128, 128), F32)
    mixed, d_records, grad_time, grad_fibre = pl.pallas_call(
        functools.partial(kernel, factor),
        out_shape=(field, field, grad, grad),
        in_specs=[any_space] * 4,
        out_specs=(any_space, any_space, vmem, vmem),
        scratch_shapes=[
            pltpu.VMEM((16, 512, 128), BF),
            pltpu.VMEM((24, 512, 128), BF),
            pltpu.VMEM((24, 512, 128), BF),
            pltpu.VMEM((36, 128, 256), BF),
            pltpu.VMEM((36, 256, 128), BF),
            pltpu.VMEM((12, 256, 512), BF),
            pltpu.VMEM((36, 128, 256), BF),
            pltpu.VMEM((32, 128, 256), F32),
            pltpu.VMEM((16, 512, 128), BF),
            pltpu.VMEM((16, 512, 128), BF),
            pltpu.VMEM((2, 9, 128, 128), BF),
            pltpu.VMEM((4, 1280, 256), BF),
            pltpu.VMEM((2, 1280, 256), F32),
            pltpu.VMEM((2, 9, 128, 128), F32),
            pltpu.VMEM((9, 128, 128), F32),
            pltpu.VMEM((members, height, 128), BF),
            pltpu.VMEM((members, height, 128), BF),
            pltpu.VMEM((nf, used, 128), F32),
            pltpu.VMEM((2, members, height, 128), BF),
            dma((8,)),
            dma((2, CHUNKS)), dma((2, CHUNKS)), dma((2, CHUNKS)), dma((2, CHUNKS)),
            dma((2, 1)), dma((2, 1)), dma((2, 1)), dma((2, 1)),
            dma((2,)), dma((members,)), dma((members,)), dma((nf,)), dma((nf,)), dma((members,)), dma((members,)),
            dma((2,)),
        ],
        compiler_params=pltpu.CompilerParams(
            collective_id=0, has_side_effects=True, vmem_limit_bytes=56 << 20
        ),
        cost_estimate=pl.CostEstimate(flops=16 * 10**9, bytes_accessed=10**7, transcendentals=10**6),
        name="block",
    )(records[0], time_weight, fibre_weight, cotangent[0])
    return mixed[None], d_records[None], grad_time, grad_fibre


def solution(mesh):
    spec = P("rep", "fibre", "tm", None)
    total = 8 * 64 * 2048
    return jax.shard_map(
        functools.partial(shards, float(total) ** -0.5),
        mesh=mesh,
        in_specs=(spec, P(), P(), spec),
        out_specs=(spec, spec, P(), P()),
        check_vma=False,
    )
```

profile of v0, /device:TPU:1, one launch (start us, length us, event | category | flops | bytes accessed | tf_op | source)
XLA Modules:
  0.0 58.3 jit_solution(11861814651682901183)
XLA Ops:
  0.6 51.3 %block.1 = (bf16[16,512,128]{2,1,0:T(8,128)(2,1)}, bf16[16,512,128]{2,1,0:T(8,128)(2,1)}, f32[9,128,128]{2,1,0:T(8,128)}, f32[9,128,128]{2,1,0:T(8,128)}) custom-call(bf16[16,512,128]{2,1,0:T(8,128)(2,1)} %bitcast.6, bf16[9,128,128]{2,1,0:T(8,128)(2,1)} %tw_hbm.1, bf16[9,128,128]{2,1,0:T(8,128)(2,1)} %fw_hbm.1, bf16[16,512,128]{2,1,0:T(8,128)(2,1)} %bitcast.7), custom_call_target="tpu_custom_call" | custom-call | flops 16000000000 | bytes 10000000 | tf_op jit(solution)/shard_map/block/pallas_call | solution.py:359
  51.9 0.0 copy-start
  51.9 3.3 %copy.12 = bf16[1,16,512,128]{3,2,1,0:T(8,128)(2,1)} copy(bf16[1,16,512,128]{3,2,1,0:T(8,128)(2,1)} %bitcast.5) | data formatting | bytes 4194304
  55.2 0.0 copy-done
  55.2 0.0 copy-start.2
  55.2 0.0 copy-start.1
  55.2 1.3 %copy.13 = bf16[1,16,512,128]{3,2,1,0:T(8,128)(2,1)} copy(bf16[1,16,512,128]{3,2,1,0:T(8,128)(2,1)S(1)} %bitcast.4) | data formatting | bytes 4194304
  56.5 0.1 copy-done.2
  56.6 0.8 %copy.14 = f32[9,128,128]{2,1,0:T(8,128)} copy(f32[9,128,128]{2,1,0:T(8,128)S(1)} %copy-done.2) | data formatting | bytes 1179648
  57.5 0.0 copy-done.1
  57.5 0.8 %copy.15 = f32[9,128,128]{2,1,0:T(8,128)} copy(f32[9,128,128]{2,1,0:T(8,128)S(1)} %copy-done.1) | data formatting | bytes 1179648
Async XLA Ops:
  51.9 3.3 %copy-start = (bf16[16,512,128]{2,1,0:T(8,128)(2,1)S(1)}, bf16[16,512,128]{2,1,0:T(8,128)(2,1)}, u32[]{:S(2)}) copy-start(bf16[16,512,128]{2,1,0:T(8,128)(2,1)} %get-tuple-element.9) | copy-start | bytes 6291460
  55.2 1.4 %copy-start.2 = (f32[9,128,128]{2,1,0:T(8,128)S(1)}, f32[9,128,128]{2,1,0:T(8,128)}, u32[]{:S(2)}) copy-start(f32[9,128,128]{2,1,0:T(8,128)} %get-tuple-element.18) | copy-start | bytes 1769476
  55.2 2.3 %copy-start.1 = (f32[9,128,128]{2,1,0:T(8,128)S(1)}, f32[9,128,128]{2,1,0:T(8,128)}, u32[]{:S(2)}) copy-start(f32[9,128,128]{2,1,0:T(8,128)} %get-tuple-element.19) | copy-start | bytes 1769476
where the time goes:
time: 58.4 us; the launch traced here: 58.3 us
  Pallas kernels  51.3 us (88%)
  local copies, waits for them, and re-layouts  6.34 us (11%)
  between operations  0.65 us (1%)
    pallas_call x1, Pallas kernels, shards(): pl.pallas_call(functools.partial(kernel, factor), out_shape=(field, field...  51.3 us
    unnamed x10, local copies, waits for them, and re-layouts  6.34 us

commit v1 on v0

--- a/solution.py
+++ b/solution.py
@@ -10,8 +10,10 @@
 MESH = pl.DeviceIdType.MESH
 BF, F32 = jnp.bfloat16, jnp.float32
 TILE = 4
-UNROLL = 2
-CHUNKS = 4
+SPANS = (slice(0, 128), slice(128, 256), slice(256, 384), slice(384, 512))
+CHUNKS = len(SPANS)
+EDGES = (0, 1, 6, 7)
+WIRE = BF
 
 
 def dot(a, b):
@@ -19,7 +21,7 @@
 
 
 def loop(low, high, body):
-    lax.fori_loop(low, high, lambda i, c: (body(i), c)[1], 0, unroll=min(UNROLL, high - low))
+    lax.fori_loop(low, high, lambda i, c: (body(i), c)[1], 0, unroll=high - low)
 
 
 def aligned(index, size):
@@ -52,11 +54,6 @@
     return dot(jnp.concatenate(lhs, axis=1), w[...])
 
 
-def fibre_conv(src, w, pair, at):
-    v = src[pl.ds(2 * pair, 10), at, :]
-    return dot(jnp.concatenate([v[i] for i in range(10)], axis=1), w[...])
-
-
 def do_hidden(xt, w, h, slope, q0):
     y = time_conv(xt, w, q0)
     s = 0.5 * jnp.tanh(0.5 * y) + 0.5
@@ -66,22 +63,45 @@
         h[4:20, aligned(q0 + j, 16), :] = natural(hid[128 * j : 128 * j + 128]).astype(BF)
 
 
-def do_d_pre(g, w, slope, dp, pair, chunk, span):
-    y = fibre_conv(g, w, pair, aligned(chunk, span)).reshape(span // 8, 8, 256)
-    z = jnp.concatenate([y[:, :, :128], y[:, :, 128:]], axis=1).reshape(span // 16, 2, 16, 128)
-    z = jnp.concatenate([z[:, 0], z[:, 1]], axis=2)
-    rows, q0 = aligned(pair, 16), chunk * (span // 16)
-    dp[pl.ds(2 + q0, span // 16), rows, :] = (z * slope[pl.ds(q0, span // 16), rows, :]).astype(BF)
+def fibre_rows(src, items):
+    return jnp.concatenate(
+        [jnp.concatenate([src[2 * p + i, at] for i in range(10)], axis=1) for p, at in items], axis=0
+    )
+
+
+def split_rows(y, items):
+    low = 0
+    for p, at in items:
+        size = at.stop - at.start
+        yield p, at, size, y[low : low + size]
+        low += size
+
+
+def do_d_pre(g, w, slope, dp, items):
+    for p, at, size, z in split_rows(dot(fibre_rows(g, items), w[...]), items):
+        count, q0 = size // 16, at.start // 16
+        z = z.reshape(size // 8, 8, 256)
+        z = jnp.concatenate([z[:, :, :128], z[:, :, 128:]], axis=1).reshape(count, 2, 16, 128)
+        z = jnp.concatenate([z[:, 0], z[:, 1]], axis=2)
+        rows = aligned(p, 16)
+        dp[2 + q0 : 2 + q0 + count, rows, :] = (z * slope[q0 : q0 + count, rows, :]).astype(BF)
+
+
+def do_grad_fibre(gt, h, acc, items):
+    lhs = [gt[pl.ds(p, 5), :, at].reshape(1280, at.stop - at.start) for p, at in items]
+    rhs = [jnp.concatenate([h[4 + 2 * p, at], h[5 + 2 * p, at]], axis=1) for p, at in items]
+    acc[...] += dot(jnp.concatenate(lhs, axis=1), jnp.concatenate(rhs, axis=0))
+
+
+def do_mixed(h, w, x, out, items):
+    for p, at, size, z in split_rows(dot(fibre_rows(h, items), w[...]), items):
+        out[2 * p, at] = (x[2 * p, at].astype(F32) + z[:, :128]).astype(BF)
+        out[2 * p + 1, at] = (x[2 * p + 1, at].astype(F32) + z[:, 128:]).astype(BF)
 
 
 def do_grad_time(xtt, dp, acc, q0, count):
     lhs = [jnp.concatenate([xtt[q0 + b + j] for j in range(count)], axis=1) for b in range(5)]
     acc[...] += dot(jnp.concatenate(lhs, axis=0), dp[pl.ds(2 + q0, count)].reshape(count * 128, 256))
-
-
-def do_grad_fibre(gt, h, acc, pair):
-    lhs = gt[pl.ds(pair, 5)].reshape(1280, gt.shape[2])
-    acc[...] += dot(lhs, jnp.concatenate([h[4 + 2 * pair], h[5 + 2 * pair]], axis=1))
 
 
 def do_d_records(dp, w, g, out, q0):
@@ -89,12 +109,6 @@
     for j in range(TILE):
         at = aligned(q0 + j, 16)
         out[:, at, :] = (g[4:20, at, :].astype(F32) + natural(y[128 * j : 128 * j + 128])).astype(BF)
-
-
-def do_mixed(h, w, x, out, pair, at):
-    y = fibre_conv(h, w, pair, at)
-    out[2 * pair, at] = (x[2 * pair, at].astype(F32) + y[:, :128]).astype(BF)
-    out[2 * pair + 1, at] = (x[2 * pair + 1, at].astype(F32) + y[:, 128:]).astype(BF)
 
 
 def fold(acc, grads):
@@ -111,10 +125,10 @@
             grads[1, k] = (part(1, (9 - k) // 2, 0, 1) + part(1, (7 - k) // 2, 1, 0)).T
 
 
-def kernel(factor, x_hbm, tw_hbm, fw_hbm, g_hbm, mixed, d_rec, gt_out, gf_out,
-           x, g, h, xt, xtt, gt, dp, slope, mix, drec, wraw, big, acc, grads, other, parts, inbox, planes, gathered,
+def kernel(factor, x_hbm, tw_hbm, fw_hbm, g_hbm, mix, drec, gathered,
+           x, g, h, xt, xtt, gt, dp, slope, wraw, big, acc, grads, other, parts, inbox, planes,
            lsem, gsend, grecv, hsend, hrecv, xsend, xrecv, dsend, drecv, asem, bsend, brecv, csend, crecv, esend, erecv,
-           fsem):
+           fsend, frecv):
     fi, ti, ri = lax.axis_index("fibre"), lax.axis_index("tm"), lax.axis_index("rep")
     nf, nt, nr = lax.axis_size("fibre"), lax.axis_size("tm"), lax.axis_size("rep")
     core = lax.rem(ti, 2)
@@ -146,8 +160,6 @@
     others += [member(lax.rem(me + d, members)) for d in range(1, members)]
     for d in others:
         pl.semaphore_signal(barrier, inc=1, device_id=d, device_id_type=MESH)
-    pl.semaphore_wait(barrier, len(others))
-
     class Halo:
         def __init__(self, axis, index, count, pieces, send, recv):
             self.has = (index < count - 1, index > 0)
@@ -170,19 +182,14 @@
             for side in range(2):
                 pl.when(self.has[side])(self.copies[i][side].wait_send)
 
-    span = 512 // CHUNKS
-    times = [slice(span * i, span * i + span) for i in range(CHUNKS)]
     g_halo = Halo("fibre", fi, nf, [
-        ((g_hbm.at[12:16, at, :], g.at[0:4, at, :]), (g_hbm.at[0:4, at, :], g.at[20:24, at, :])) for at in times
+        ((g_hbm.at[12:16, at, :], g.at[0:4, at, :]), (g_hbm.at[0:4, at, :], g.at[20:24, at, :])) for at in SPANS
     ], gsend, grecv)
     h_halo = Halo("fibre", fi, nf, [
-        ((h.at[16:20, at, :], h.at[0:4, at, :]), (h.at[4:8, at, :], h.at[20:24, at, :])) for at in times
+        ((h.at[16:20, at, :], h.at[0:4, at, :]), (h.at[4:8, at, :], h.at[20:24, at, :])) for at in SPANS
     ], hsend, hrecv)
     x_halo = Halo("tm", ti, nt, [((xt.at[32:34], xt.at[0:2]), (xt.at[2:4], xt.at[34:36]))], xsend, xrecv)
     d_halo = Halo("tm", ti, nt, [((dp.at[32:34], dp.at[0:2]), (dp.at[2:4], dp.at[34:36]))], dsend, drecv)
-    for i in range(CHUNKS):
-        g_halo.start(i)
-
     def build(q):
         v = to_time_pairs(x, q)
         xt[q + 2] = v
@@ -192,7 +199,10 @@
         c.wait()
     for q in (0, 1, 30, 31):
         build(q)
+    pl.semaphore_wait(barrier, len(others))
     x_halo.start(0)
+    for i in range(CHUNKS):
+        g_halo.start(i)
 
     for edge, at, time_at in ((0, slice(0, 4), slice(0, 2)), (1, slice(20, 24), slice(34, 36))):
         @pl.when((fi == 0) if edge == 0 else (fi == nf - 1))
@@ -217,43 +227,47 @@
     pair_weights(big.at[2], lambda k: wraw[1, k])
     pair_weights(big.at[3], lambda k: wraw[0, 8 - k].T)
 
+    g_load.wait()
+
+    def turn(p, spans):
+        for at in spans:
+            gt[p, :, at] = jnp.concatenate([g[2 * p, at], g[2 * p + 1, at]], axis=1).T
+
+    acc[...] = jnp.zeros(acc.shape, F32)
+    quarters = [slice(128 * i, 128 * i + 128) for i in range(4)]
+    loop(2, 10, lambda p: turn(p, quarters))
+    inner, outer = (slice(128, 384),), (quarters[0], quarters[3])
+    loop(2, 6, lambda p: do_d_pre(g, big.at[1], slope, dp, [(p, at) for at in inner]))
+    loop(2, 6, lambda p: do_grad_fibre(gt, h, acc.at[1], [(p, at) for at in inner]))
+
     x_halo.wait_recv(0)
     for q in (0, 1, 34, 35):
         xtt[q] = xt[q].T
     do_hidden(xt, big.at[0], h, slope, last * TILE)
     do_hidden(xt, big.at[0], h, slope, 0)
-
-    g_load.wait()
-
-    def turn(p):
-        for at in (slice(0, 128), slice(128, 256), slice(256, 384), slice(384, 512)):
-            gt[p, :, at] = jnp.concatenate([g[2 * p, at], g[2 * p + 1, at]], axis=1).T
-
-    acc[...] = jnp.zeros(acc.shape, F32)
-    loop(2, 10, turn)
-    loop(2, 6, lambda p: do_d_pre(g, big.at[1], slope, dp, p, 0, 512))
-    loop(2, 6, lambda p: do_grad_fibre(gt, h, acc.at[1], p))
-    loop(2, 6, lambda p: do_mixed(h, big.at[2], x, mix, p, slice(0, 512)))
-
-    for i in range(CHUNKS):
+    loop(2, 6, lambda p: do_d_pre(g, big.at[1], slope, dp, [(p, at) for at in outer]))
+    loop(2, 6, lambda p: do_grad_fibre(gt, h, acc.at[1], [(p, at) for at in outer]))
+
+    for i, at in enumerate(SPANS):
         g_halo.wait_recv(i)
-    for i in range(CHUNKS):
-        h_halo.start(i)
-    for p in (0, 1, 6, 7):
-        do_d_pre(g, big.at[1], slope, dp, p, 0, 512)
-    d_halo.start(0)
-    loop(0, 8, lambda i: do_grad_time(xtt, dp, acc.at[0], 4 * i, 4))
-    for p in (0, 1, 10, 11):
-        turn(p)
-    for p in (0, 1, 6, 7):
-        do_grad_fibre(gt, h, acc.at[1], p)
+        if i == CHUNKS - 1:
+            for j in range(CHUNKS):
+                h_halo.start(j)
+        items = [(p, at) for p in EDGES]
+        do_d_pre(g, big.at[1], slope, dp, items)
+        if i == CHUNKS - 1:
+            d_halo.start(0)
+        for p in (0, 1, 10, 11):
+            turn(p, [at])
+        do_grad_fibre(gt, h, acc.at[1], items)
+        loop(at.start // 64, at.stop // 64, lambda q: do_grad_time(xtt, dp, acc.at[0], 4 * q, 4))
     fold(acc, grads)
 
     swap = pltpu.make_async_remote_copy(
         src_ref=grads.at[1 - core], dst_ref=other, send_sem=asem.at[0], recv_sem=asem.at[1],
         device_id=partner, device_id_type=MESH)
     swap.start()
-    loop(1, last, lambda i: do_d_records(dp, big.at[3], g, drec, i * TILE))
+    loop(2, 6, lambda p: do_mixed(h, big.at[2], x, mix, [(p, slice(0, 512))]))
     swap.wait_recv()
 
     pad = jnp.zeros((parts.shape[1] - used, 128), F32) if parts.shape[1] > used else None
@@ -263,7 +277,7 @@
 
     for s in range(members):
         at = slice(rows * s, rows * s + rows)
-        parts[s] = padded((grads[core, :, at] + other[:, at]).reshape(used, 128)).astype(BF)
+        parts[s] = padded((grads[core, :, at] + other[:, at]).reshape(used, 128)).astype(WIRE)
     mine = aligned(me, rows)
     own = (grads[core, :, mine] + other[:, mine]).reshape(used, 128)
     scatter = []
@@ -275,12 +289,7 @@
     for c in scatter:
         c.start()
 
-    d_halo.wait_recv(0)
-    do_d_records(dp, big.at[3], g, drec, last * TILE)
-    do_d_records(dp, big.at[3], g, drec, 0)
-    out_d = pltpu.make_async_copy(drec, d_rec, lsem.at[6])
-    out_d.start()
-
+    loop(1, last, lambda i: do_d_records(dp, big.at[3], g, drec, i * TILE))
     for d, c in enumerate(scatter, 1):
         c.wait_recv()
         own = own + inbox[d].astype(F32)[:used]
@@ -294,8 +303,9 @@
     for c in spread:
         c.start()
 
-    for p in (0, 1, 6, 7):
-        pass
+    d_halo.wait_recv(0)
+    do_d_records(dp, big.at[3], g, drec, last * TILE)
+    do_d_records(dp, big.at[3], g, drec, 0)
     for d in range(1, nf):
         source = lax.rem(fi - d + nf, nf)
         pltpu.make_async_remote_copy(
@@ -313,38 +323,33 @@
     for c in gather:
         c.start()
 
+    def forward(which, part, d):
+        return pltpu.make_async_remote_copy(
+            src_ref=gathered.at[which, part], dst_ref=gathered.at[which, part], send_sem=fsend.at[d],
+            recv_sem=frecv.at[d], device_id=partner, device_id_type=MESH)
+
+    passed = [forward(core, me, 0)]
+    passed[0].start()
     for i in range(CHUNKS):
         h_halo.wait_recv(i)
-        for p in (0, 1, 6, 7):
-            do_mixed(h, big.at[2], x, mix, p, times[i])
-    out_m = pltpu.make_async_copy(mix, mixed, lsem.at[7])
-    out_m.start()
+        do_mixed(h, big.at[2], x, mix, [(p, SPANS[i]) for p in EDGES])
 
     for d in range(1, members):
         source = lax.rem(me - d + members, members)
         pltpu.make_async_remote_copy(
             src_ref=gathered.at[core, source], dst_ref=gathered.at[core, source], send_sem=esend.at[d],
             recv_sem=erecv.at[d], device_id=member(source), device_id_type=MESH).wait_recv()
-    final = pltpu.make_async_remote_copy(
-        src_ref=gathered.at[core], dst_ref=gathered.at[core], send_sem=fsem.at[0], recv_sem=fsem.at[1],
-        device_id=partner, device_id_type=MESH)
-    final.start()
-    final.wait_send()
-    pltpu.make_async_remote_copy(
-        src_ref=gathered.at[1 - core], dst_ref=gathered.at[1 - core], send_sem=fsem.at[0], recv_sem=fsem.at[1],
-        device_id=partner, device_id_type=MESH).wait_recv()
-    for i, out in enumerate((gt_out, gf_out)):
-        for s in range(members):
-            out[:, rows * s : rows * s + rows] = gathered[i, s].astype(F32)[:used].reshape(9, rows, 128)
+        passed.append(forward(core, source, d))
+        passed[-1].start()
+    for d in range(members):
+        forward(1 - core, lax.rem(me - d + members, members), d).wait_recv()
 
     swap.wait_send()
-    for c in (*scatter, *spread, *gather):
+    for c in (*scatter, *spread, *gather, *passed):
         c.wait_send()
     for halo, count in ((g_halo, CHUNKS), (h_halo, CHUNKS), (x_halo, 1), (d_halo, 1)):
         for i in range(count):
             halo.wait_send(i)
-    out_d.wait()
-    out_m.wait()
 
 
 def shards(factor, records, time_weight, fibre_weight, cotangent):
@@ -353,14 +358,14 @@
     used = 9 * (128 // members)
     height = -(-used // 16) * 16
     dma = pltpu.SemaphoreType.DMA
-    any_space, vmem = pl.BlockSpec(memory_space=pl.ANY), pl.BlockSpec(memory_space=pltpu.VMEM)
-    field = jax.ShapeDtypeStruct((16, 512, 128), BF)
-    grad = jax.ShapeDtypeStruct((9, 128, 128), F32)
-    mixed, d_records, grad_time, grad_fibre = pl.pallas_call(
+    any_space = pl.BlockSpec(memory_space=pl.ANY)
+    mix, drec, gathered = pl.pallas_call(
         functools.partial(kernel, factor),
-        out_shape=(field, field, grad, grad),
-        in_specs=[any_space] * 4,
-        out_specs=(any_space, any_space, vmem, vmem),
+        out_shape=(
+            pltpu.VMEM((16, 512, 128), BF), pltpu.VMEM((16, 512, 128), BF), pltpu.VMEM((2, members, height, 128), BF)
+        ),
+        in_specs=[pl.BlockSpec(memory_space=pltpu.HBM)] * 4,
+        out_specs=(pl.BlockSpec(memory_space=pltpu.VMEM),) * 3,
         scratch_shapes=[
             pltpu.VMEM((16, 512, 128), BF),
             pltpu.VMEM((24, 512, 128), BF),
@@ -370,29 +375,52 @@
             pltpu.VMEM((12, 256, 512), BF),
             pltpu.VMEM((36, 128, 256), BF),
             pltpu.VMEM((32, 128, 256), F32),
-            pltpu.VMEM((16, 512, 128), BF),
-            pltpu.VMEM((16, 512, 128), BF),
             pltpu.VMEM((2, 9, 128, 128), BF),
             pltpu.VMEM((4, 1280, 256), BF),
             pltpu.VMEM((2, 1280, 256), F32),
             pltpu.VMEM((2, 9, 128, 128), F32),
             pltpu.VMEM((9, 128, 128), F32),
-            pltpu.VMEM((members, height, 128), BF),
-            pltpu.VMEM((members, height, 128), BF),
+            pltpu.VMEM((members, height, 128), WIRE),
+            pltpu.VMEM((members, height, 128), WIRE),
             pltpu.VMEM((nf, used, 128), F32),
-            pltpu.VMEM((2, members, height, 128), BF),
             dma((8,)),
             dma((2, CHUNKS)), dma((2, CHUNKS)), dma((2, CHUNKS)), dma((2, CHUNKS)),
             dma((2, 1)), dma((2, 1)), dma((2, 1)), dma((2, 1)),
             dma((2,)), dma((members,)), dma((members,)), dma((nf,)), dma((nf,)), dma((members,)), dma((members,)),
-            dma((2,)),
+            dma((members,)), dma((members,)),
         ],
         compiler_params=pltpu.CompilerParams(
-            collective_id=0, has_side_effects=True, vmem_limit_bytes=56 << 20
+            collective_id=0, has_side_effects=True, vmem_limit_bytes=48 << 20
         ),
         cost_estimate=pl.CostEstimate(flops=16 * 10**9, bytes_accessed=10**7, transcendentals=10**6),
         name="block",
-    )(records[0], time_weight, fibre_weight, cotangent[0])
+    )(*(pltpu.with_memory_space_constraint(a, pltpu.HBM) for a in (records[0], time_weight, fibre_weight, cotangent[0])))
+
+    def store(mix, drec, gathered, mixed, d_records, grad_time, grad_fibre, staged, sem):
+        copies = [pltpu.make_async_copy(mix, mixed, sem.at[0]), pltpu.make_async_copy(drec, d_records, sem.at[1])]
+        for c in copies:
+            c.start()
+        rows = 128 // members
+        for i, out in enumerate((grad_time, grad_fibre)):
+            for s in range(members):
+                staged[i, :, rows * s : rows * s + rows] = gathered[i, s].astype(F32)[:used].reshape(9, rows, 128)
+            copies.append(pltpu.make_async_copy(staged.at[i], out, sem.at[2 + i]))
+            copies[-1].start()
+        for c in copies:
+            c.wait()
+
+    field = jax.ShapeDtypeStruct((16, 512, 128), BF)
+    grad = jax.ShapeDtypeStruct((9, 128, 128), F32)
+    mixed, d_records, grad_time, grad_fibre = pl.pallas_call(
+        store,
+        out_shape=(field, field, grad, grad),
+        in_specs=[any_space, any_space, pl.BlockSpec(memory_space=pltpu.VMEM)],
+        out_specs=(any_space,) * 4,
+        scratch_shapes=[pltpu.VMEM((2, 9, 128, 128), F32), dma((4,))],
+        compiler_params=pltpu.CompilerParams(vmem_limit_bytes=8 << 20),
+        cost_estimate=pl.CostEstimate(flops=0, bytes_accessed=10**7, transcendentals=0),
+        name="store",
+    )(mix, drec, gathered)
     return mixed[None], d_records[None], grad_time, grad_fibre
 
 

time: 58.4 us -> 52.2 us (0.89)
  local copies, waits for them, and re-layouts: 6.34 us -> 0 us
    unnamed x10 -> x0, local copies, waits for them, and re-layouts: 6.34 us -> none
    pallas_call x1 -> x2, Pallas kernels: 51.3 us -> 51.3 us  [the longest x1 48.9 us: shards(): pl.pallas_call(functools.partial(kernel, factor), out_shape=(pltpu.VMEM((...]
where the time goes in v1:
time: 52.2 us; the launch traced here: 52.1 us
  Pallas kernels  51.3 us (98%)
  between operations  0.8 us (2%)
    pallas_call x1, Pallas kernels, shards(): pl.pallas_call(functools.partial(kernel, factor), out_shape=(pltpu.VMEM((...  48.9 us
    pallas_call x1, Pallas kernels, shards(): pl.pallas_call(store, out_shape=(field, field, grad, grad), in_specs=[any...  2.41 us

profile of v1, /device:TPU:1, one launch (start us, length us, event | category | flops | bytes accessed | tf_op | source)
XLA Modules:
  0.0 52.1 jit_solution(17334452054841607230)
XLA Ops:
  0.6 48.9 %block.1 = (bf16[16,512,128]{2,1,0:T(8,128)(2,1)S(1)}, bf16[16,512,128]{2,1,0:T(8,128)(2,1)S(1)}, bf16[2,16,80,128]{3,2,1,0:T(8,128)(2,1)S(1)}) custom-call(bf16[16,512,128]{2,1,0:T(8,128)(2,1)} %bitcast.4, bf16[9,128,128]{2,1,0:T(8,128)(2,1)} %tw_hbm.1, bf16[9,128,128]{2,1,0:T(8,128)(2,1)} %fw_hbm.1, bf16[16,512,128]{2,1,0:T(8,128)(2,1)} %bitcast.5), custom_call_target="tpu_custom_call" | custom-call | flops 16000000000 | bytes 10000000 | tf_op jit(solution)/shard_map/block/pallas_call | solution.py:362
  49.5 2.4 %store.1 = (bf16[16,512,128]{2,1,0:T(8,128)(2,1)}, bf16[16,512,128]{2,1,0:T(8,128)(2,1)}, f32[9,128,128]{2,1,0:T(8,128)}, f32[9,128,128]{2,1,0:T(8,128)}) custom-call(bf16[16,512,128]{2,1,0:T(8,128)(2,1)S(1)} %get-tuple-element.11.mix, bf16[16,512,128]{2,1,0:T(8,128)(2,1)S(1)} %get-tuple-element.12.drec, bf16[2,16,80,128]{3,2,1,0:T(8,128)(2,1)S(1)} %get-tuple-element.13.gathered), custom_call_target="tpu_custom_call" | custom-call | bytes 10000000 | tf_op jit(solution)/shard_map/store/pallas_call | solution.py:414

commit v2 on v1

--- a/solution.py
+++ b/solution.py
@@ -10,7 +10,7 @@
 MESH = pl.DeviceIdType.MESH
 BF, F32 = jnp.bfloat16, jnp.float32
 TILE = 4
-SPANS = (slice(0, 128), slice(128, 256), slice(256, 384), slice(384, 512))
+SPANS = (slice(0, 256), slice(256, 512))
 CHUNKS = len(SPANS)
 EDGES = (0, 1, 6, 7)
 WIRE = BF
@@ -128,7 +128,7 @@
 def kernel(factor, x_hbm, tw_hbm, fw_hbm, g_hbm, mix, drec, gathered,
            x, g, h, xt, xtt, gt, dp, slope, wraw, big, acc, grads, other, parts, inbox, planes,
            lsem, gsend, grecv, hsend, hrecv, xsend, xrecv, dsend, drecv, asem, bsend, brecv, csend, crecv, esend, erecv,
-           fsend, frecv):
+           fsem):
     fi, ti, ri = lax.axis_index("fibre"), lax.axis_index("tm"), lax.axis_index("rep")
     nf, nt, nr = lax.axis_size("fibre"), lax.axis_size("tm"), lax.axis_size("rep")
     core = lax.rem(ti, 2)
@@ -137,6 +137,11 @@
     rows = 128 // members
     used = 9 * rows
 
+    offsets = sorted(range(1, members), key=lambda d: -sum(min(i, 4 - i) for i in (d // 4, d % 4)))
+
+    def moved(d, sign):
+        return 4 * lax.rem(me // 4 + sign * (d // 4) + members, members // 4) + lax.rem(me % 4 + sign * (d % 4) + 4, 4)
+
     def member(index):
         return {"tm": 2 * lax.div(index, nr) + core, "rep": lax.rem(index, nr)}
 
@@ -144,6 +149,13 @@
         return {axis: lax.rem(index + step + count, count)}
 
     partner = {"tm": ti + 1 - 2 * core}
+
+    barrier = pltpu.get_barrier_semaphore()
+    others = [shifted("fibre", fi, nf, d) for d in range(1, nf)]
+    others += [shifted("tm", ti, nt, d) for d in (1, -1)]
+    others = [member(moved(d, 1)) for d in offsets] + others
+    for d in others:
+        pl.semaphore_signal(barrier, inc=1, device_id=d, device_id_type=MESH)
 
     x_edges = [pltpu.make_async_copy(x_hbm.at[:, at, :], x.at[:, at, :], lsem.at[i])
                for i, at in enumerate((slice(0, 32), slice(480, 512)))]
@@ -154,12 +166,6 @@
     for c in (*x_edges, w_time, x_rest, w_fibre, g_load):
         c.start()
 
-    barrier = pltpu.get_barrier_semaphore()
-    others = [shifted("fibre", fi, nf, d) for d in range(1, nf)]
-    others += [shifted("tm", ti, nt, d) for d in (1, -1)]
-    others += [member(lax.rem(me + d, members)) for d in range(1, members)]
-    for d in others:
-        pl.semaphore_signal(barrier, inc=1, device_id=d, device_id_type=MESH)
     class Halo:
         def __init__(self, axis, index, count, pieces, send, recv):
             self.has = (index < count - 1, index > 0)
@@ -195,14 +201,14 @@
         xt[q + 2] = v
         xtt[q + 2] = v.T
 
+    pl.semaphore_wait(barrier, len(others))
+    for i in range(CHUNKS):
+        g_halo.start(i)
     for c in x_edges:
         c.wait()
     for q in (0, 1, 30, 31):
         build(q)
-    pl.semaphore_wait(barrier, len(others))
     x_halo.start(0)
-    for i in range(CHUNKS):
-        g_halo.start(i)
 
     for edge, at, time_at in ((0, slice(0, 4), slice(0, 2)), (1, slice(20, 24), slice(34, 36))):
         @pl.when((fi == 0) if edge == 0 else (fi == nf - 1))
@@ -281,8 +287,8 @@
     mine = aligned(me, rows)
     own = (grads[core, :, mine] + other[:, mine]).reshape(used, 128)
     scatter = []
-    for d in range(1, members):
-        to = lax.rem(me + d, members)
+    for d in offsets:
+        to = moved(d, 1)
         scatter.append(pltpu.make_async_remote_copy(
             src_ref=parts.at[to], dst_ref=inbox.at[d], send_sem=bsend.at[d], recv_sem=brecv.at[d],
             device_id=member(to), device_id_type=MESH))
@@ -290,7 +296,7 @@
         c.start()
 
     loop(1, last, lambda i: do_d_records(dp, big.at[3], g, drec, i * TILE))
-    for d, c in enumerate(scatter, 1):
+    for d, c in zip(offsets, scatter):
         c.wait_recv()
         own = own + inbox[d].astype(F32)[:used]
     planes[fi] = own
@@ -316,36 +322,34 @@
         total = total + planes[i]
     gathered[core, me] = padded(total * factor).astype(BF)
     gather = []
-    for d in range(1, members):
+    for d in offsets:
         gather.append(pltpu.make_async_remote_copy(
             src_ref=gathered.at[core, me], dst_ref=gathered.at[core, me], send_sem=esend.at[d], recv_sem=erecv.at[d],
-            device_id=member(lax.rem(me + d, members)), device_id_type=MESH))
+            device_id=member(moved(d, 1)), device_id_type=MESH))
     for c in gather:
         c.start()
 
-    def forward(which, part, d):
-        return pltpu.make_async_remote_copy(
-            src_ref=gathered.at[which, part], dst_ref=gathered.at[which, part], send_sem=fsend.at[d],
-            recv_sem=frecv.at[d], device_id=partner, device_id_type=MESH)
-
-    passed = [forward(core, me, 0)]
-    passed[0].start()
     for i in range(CHUNKS):
         h_halo.wait_recv(i)
         do_mixed(h, big.at[2], x, mix, [(p, SPANS[i]) for p in EDGES])
 
-    for d in range(1, members):
-        source = lax.rem(me - d + members, members)
+    for d in offsets:
+        source = moved(d, -1)
         pltpu.make_async_remote_copy(
             src_ref=gathered.at[core, source], dst_ref=gathered.at[core, source], send_sem=esend.at[d],
             recv_sem=erecv.at[d], device_id=member(source), device_id_type=MESH).wait_recv()
-        passed.append(forward(core, source, d))
-        passed[-1].start()
-    for d in range(members):
-        forward(1 - core, lax.rem(me - d + members, members), d).wait_recv()
-
+
+    def forward(which):
+        return pltpu.make_async_remote_copy(
+            src_ref=gathered.at[which], dst_ref=gathered.at[which], send_sem=fsem.at[0],
+            recv_sem=fsem.at[1], device_id=partner, device_id_type=MESH)
+
+    forward(core).start()
+    forward(1 - core).wait_recv()
+
+    forward(core).wait_send()
     swap.wait_send()
-    for c in (*scatter, *spread, *gather, *passed):
+    for c in (*scatter, *spread, *gather):
         c.wait_send()
     for halo, count in ((g_halo, CHUNKS), (h_halo, CHUNKS), (x_halo, 1), (d_halo, 1)):
         for i in range(count):
@@ -387,7 +391,7 @@
             dma((2, CHUNKS)), dma((2, CHUNKS)), dma((2, CHUNKS)), dma((2, CHUNKS)),
             dma((2, 1)), dma((2, 1)), dma((2, 1)), dma((2, 1)),
             dma((2,)), dma((members,)), dma((members,)), dma((nf,)), dma((nf,)), dma((members,)), dma((members,)),
-            dma((members,)), dma((members,)),
+            dma((2,)),
         ],
         compiler_params=pltpu.CompilerParams(
             collective_id=0, has_side_effects=True, vmem_limit_bytes=48 << 20

time: 52.2 us -> 50.7 us (0.971)
  Pallas kernels: 51.3 us -> 49.8 us
    pallas_call x1, Pallas kernels: 48.9 us -> 47.4 us  [shards(): pl.pallas_call(functools.partial(kernel, factor), out_shape=(pltpu.VMEM((...]
where the time goes in v2:
time: 50.7 us; the launch traced here: 50.6 us
  Pallas kernels  49.8 us (98%)
  between operations  0.8 us (2%)
    pallas_call x1, Pallas kernels, shards(): pl.pallas_call(functools.partial(kernel, factor), out_shape=(pltpu.VMEM((...  47.4 us
    pallas_call x1, Pallas kernels, shards(): pl.pallas_call(store, out_shape=(field, field, grad, grad), in_specs=[any...  2.41 us

profile of v2, /device:TPU:1, one launch (start us, length us, event | category | flops | bytes accessed | tf_op | source)
XLA Modules:
  0.0 50.6 jit_solution(6901641381302962879)
XLA Ops:
  0.6 47.4 %block.1 = (bf16[16,512,128]{2,1,0:T(8,128)(2,1)S(1)}, bf16[16,512,128]{2,1,0:T(8,128)(2,1)S(1)}, bf16[2,16,80,128]{3,2,1,0:T(8,128)(2,1)S(1)}) custom-call(bf16[16,512,128]{2,1,0:T(8,128)(2,1)} %bitcast.4, bf16[9,128,128]{2,1,0:T(8,128)(2,1)} %tw_hbm.1, bf16[9,128,128]{2,1,0:T(8,128)(2,1)} %fw_hbm.1, bf16[16,512,128]{2,1,0:T(8,128)(2,1)} %bitcast.5), custom_call_target="tpu_custom_call" | custom-call | flops 16000000000 | bytes 10000000 | tf_op jit(solution)/shard_map/block/pallas_call | solution.py:366
  48.0 2.4 %store.1 = (bf16[16,512,128]{2,1,0:T(8,128)(2,1)}, bf16[16,512,128]{2,1,0:T(8,128)(2,1)}, f32[9,128,128]{2,1,0:T(8,128)}, f32[9,128,128]{2,1,0:T(8,128)}) custom-call(bf16[16,512,128]{2,1,0:T(8,128)(2,1)S(1)} %get-tuple-element.11.mix, bf16[16,512,128]{2,1,0:T(8,128)(2,1)S(1)} %get-tuple-element.12.drec, bf16[2,16,80,128]{3,2,1,0:T(8,128)(2,1)S(1)} %get-tuple-element.13.gathered), custom_call_target="tpu_custom_call" | custom-call | bytes 10000000 | tf_op jit(solution)/shard_map/store/pallas_call | solution.py:418

commit v3 on v2

--- a/solution.py
+++ b/solution.py
@@ -201,14 +201,14 @@
         xt[q + 2] = v
         xtt[q + 2] = v.T
 
-    pl.semaphore_wait(barrier, len(others))
-    for i in range(CHUNKS):
-        g_halo.start(i)
     for c in x_edges:
         c.wait()
     for q in (0, 1, 30, 31):
         build(q)
+    pl.semaphore_wait(barrier, len(others))
     x_halo.start(0)
+    for i in range(CHUNKS):
+        g_halo.start(i)
 
     for edge, at, time_at in ((0, slice(0, 4), slice(0, 2)), (1, slice(20, 24), slice(34, 36))):
         @pl.when((fi == 0) if edge == 0 else (fi == nf - 1))
@@ -321,23 +321,22 @@
     for i in range(1, nf):
         total = total + planes[i]
     gathered[core, me] = padded(total * factor).astype(BF)
-    gather = []
+    def piece(which, part, to):
+        return pltpu.make_async_remote_copy(
+            src_ref=gathered.at[which, part], dst_ref=gathered.at[which, part], send_sem=esend.at[to],
+            recv_sem=erecv.at[part], device_id=member(to), device_id_type=MESH)
+
+    pl.when(me != 0)(piece(core, me, 0).start)
     for d in offsets:
-        gather.append(pltpu.make_async_remote_copy(
-            src_ref=gathered.at[core, me], dst_ref=gathered.at[core, me], send_sem=esend.at[d], recv_sem=erecv.at[d],
-            device_id=member(moved(d, 1)), device_id_type=MESH))
-    for c in gather:
-        c.start()
+        to = moved(d, 1)
+        pl.when(to != 0)(piece(core, me, to).start)
 
     for i in range(CHUNKS):
         h_halo.wait_recv(i)
         do_mixed(h, big.at[2], x, mix, [(p, SPANS[i]) for p in EDGES])
 
-    for d in offsets:
-        source = moved(d, -1)
-        pltpu.make_async_remote_copy(
-            src_ref=gathered.at[core, source], dst_ref=gathered.at[core, source], send_sem=esend.at[d],
-            recv_sem=erecv.at[d], device_id=member(source), device_id_type=MESH).wait_recv()
+    for s in range(members):
+        pl.when(me != s)(piece(core, s, me).wait_recv)
 
     def forward(which):
         return pltpu.make_async_remote_copy(
@@ -349,8 +348,10 @@
 
     forward(core).wait_send()
     swap.wait_send()
-    for c in (*scatter, *spread, *gather):
+    for c in (*scatter, *spread):
         c.wait_send()
+    for s in range(members):
+        pl.when(me != s)(piece(core, me, s).wait_send)
     for halo, count in ((g_halo, CHUNKS), (h_halo, CHUNKS), (x_halo, 1), (d_halo, 1)):
         for i in range(count):
             halo.wait_send(i)

time: 50.7 us -> 50.1 us (0.988)
  Pallas kernels: 49.8 us -> 49.1 us
    pallas_call x1, Pallas kernels: 47.4 us -> 46.7 us  [shards(): pl.pallas_call(functools.partial(kernel, factor), out_shape=(pltpu.VMEM((...]
where the time goes in v3:
time: 50.1 us; the launch traced here: 49.9 us
  Pallas kernels  49.1 us (98%)
  between operations  0.8 us (2%)
    pallas_call x1, Pallas kernels, shards(): pl.pallas_call(functools.partial(kernel, factor), out_shape=(pltpu.VMEM((...  46.7 us
    pallas_call x1, Pallas kernels, shards(): pl.pallas_call(store, out_shape=(field, field, grad, grad), in_specs=[any...  2.41 us

profile of v3, /device:TPU:1, one launch (start us, length us, event | category | flops | bytes accessed | tf_op | source)
XLA Modules:
  0.0 49.9 jit_solution(1849656840966907344)
XLA Ops:
  0.6 46.7 %block.1 = (bf16[16,512,128]{2,1,0:T(8,128)(2,1)S(1)}, bf16[16,512,128]{2,1,0:T(8,128)(2,1)S(1)}, bf16[2,16,80,128]{3,2,1,0:T(8,128)(2,1)S(1)}) custom-call(bf16[16,512,128]{2,1,0:T(8,128)(2,1)} %bitcast.4, bf16[9,128,128]{2,1,0:T(8,128)(2,1)} %tw_hbm.1, bf16[9,128,128]{2,1,0:T(8,128)(2,1)} %fw_hbm.1, bf16[16,512,128]{2,1,0:T(8,128)(2,1)} %bitcast.5), custom_call_target="tpu_custom_call" | custom-call | flops 16000000000 | bytes 10000000 | tf_op jit(solution)/shard_map/block/pallas_call | solution.py:367
  47.4 2.4 %store.1 = (bf16[16,512,128]{2,1,0:T(8,128)(2,1)}, bf16[16,512,128]{2,1,0:T(8,128)(2,1)}, f32[9,128,128]{2,1,0:T(8,128)}, f32[9,128,128]{2,1,0:T(8,128)}) custom-call(bf16[16,512,128]{2,1,0:T(8,128)(2,1)S(1)} %get-tuple-element.11.mix, bf16[16,512,128]{2,1,0:T(8,128)(2,1)S(1)} %get-tuple-element.12.drec, bf16[2,16,80,128]{3,2,1,0:T(8,128)(2,1)S(1)} %get-tuple-element.13.gathered), custom_call_target="tpu_custom_call" | custom-call | bytes 10000000 | tf_op jit(solution)/shard_map/store/pallas_call | solution.py:419

commit v4 on v3

--- a/solution.py
+++ b/solution.py
@@ -281,19 +281,17 @@
     def padded(v):
         return v if pad is None else jnp.concatenate([v, pad], axis=0)
 
-    for s in range(members):
-        at = slice(rows * s, rows * s + rows)
-        parts[s] = padded((grads[core, :, at] + other[:, at]).reshape(used, 128)).astype(WIRE)
     mine = aligned(me, rows)
     own = (grads[core, :, mine] + other[:, mine]).reshape(used, 128)
     scatter = []
     for d in offsets:
         to = moved(d, 1)
+        at = aligned(to, rows)
+        parts[to] = padded((grads[core, :, at] + other[:, at]).reshape(used, 128)).astype(WIRE)
         scatter.append(pltpu.make_async_remote_copy(
             src_ref=parts.at[to], dst_ref=inbox.at[d], send_sem=bsend.at[d], recv_sem=brecv.at[d],
             device_id=member(to), device_id_type=MESH))
-    for c in scatter:
-        c.start()
+        scatter[-1].start()
 
     loop(1, last, lambda i: do_d_records(dp, big.at[3], g, drec, i * TILE))
     for d, c in zip(offsets, scatter):

time: 50.1 us -> 50 us (level)
  no operation moved by 1% of the time
where the time goes in v4:
time: 50 us; the launch traced here: 49.9 us
  Pallas kernels  49.1 us (98%)
  between operations  0.8 us (2%)
    pallas_call x1, Pallas kernels, shards(): pl.pallas_call(functools.partial(kernel, factor), out_shape=(pltpu.VMEM((...  46.7 us
    pallas_call x1, Pallas kernels, shards(): pl.pallas_call(store, out_shape=(field, field, grad, grad), in_specs=[any...  2.41 us

profile of v4, /device:TPU:1, one launch (start us, length us, event | category | flops | bytes accessed | tf_op | source)
XLA Modules:
  0.0 49.9 jit_solution(4580414152762062623)
XLA Ops:
  0.6 46.7 %block.1 = (bf16[16,512,128]{2,1,0:T(8,128)(2,1)S(1)}, bf16[16,512,128]{2,1,0:T(8,128)(2,1)S(1)}, bf16[2,16,80,128]{3,2,1,0:T(8,128)(2,1)S(1)}) custom-call(bf16[16,512,128]{2,1,0:T(8,128)(2,1)} %bitcast.4, bf16[9,128,128]{2,1,0:T(8,128)(2,1)} %tw_hbm.1, bf16[9,128,128]{2,1,0:T(8,128)(2,1)} %fw_hbm.1, bf16[16,512,128]{2,1,0:T(8,128)(2,1)} %bitcast.5), custom_call_target="tpu_custom_call" | custom-call | flops 16000000000 | bytes 10000000 | tf_op jit(solution)/shard_map/block/pallas_call | solution.py:365
  47.3 2.4 %store.1 = (bf16[16,512,128]{2,1,0:T(8,128)(2,1)}, bf16[16,512,128]{2,1,0:T(8,128)(2,1)}, f32[9,128,128]{2,1,0:T(8,128)}, f32[9,128,128]{2,1,0:T(8,128)}) custom-call(bf16[16,512,128]{2,1,0:T(8,128)(2,1)S(1)} %get-tuple-element.11.mix, bf16[16,512,128]{2,1,0:T(8,128)(2,1)S(1)} %get-tuple-element.12.drec, bf16[2,16,80,128]{3,2,1,0:T(8,128)(2,1)S(1)} %get-tuple-element.13.gathered), custom_call_target="tpu_custom_call" | custom-call | bytes 10000000 | tf_op jit(solution)/shard_map/store/pallas_call | solution.py:417
